TPU v7x, 32 devices: a whole 2x2x4 slice. The times are simulated.
32 devices in a mesh: lat: 8 (over z, core), lon: 4 (over y, x).
Axes of the slice: x: 2, y: 2, z: 4, core: 2. Of those that a mesh axis runs over, the one named last changes fastest.
Arguments:
- tokens: bfloat16 [4, 48, 96, 192], P(None, 'lat', 'lon'), may hold values from -6 to 6
- cotangent: bfloat16 [4, 48, 96, 192], P(None, 'lat', 'lon'), may hold values from -6 to 6
- norm_gain: float32 [192], replicated, may hold values from 0.1 to 1.9
- inproj_weight: bfloat16 [192, 576], replicated, may hold values from -0.4375 to 0.4375
- outproj_weight: bfloat16 [192, 192], replicated, may hold values from -0.4375 to 0.4375
- bias: float32 [2, 8, 6, 144, 144], P(None, 'lat'), may hold values from -4 to 4
Outputs:
- grad_input: bfloat16 [4, 48, 96, 192], P(None, 'lat', 'lon')
- bias_grad: float32 [2, 8, 6, 144, 144], P(None, 'lat', None, 'lon')
All inputs are finite; a program needn't handle non-finite values.
Results may differ from a plain program's by a relative error of at most 0.017.
Values may be sent and summed in bfloat16 or wider, within the bound.
No kernel may reach another device: no remote copies, remote signals or barrier semaphores. Data moves between devices by JAX's collectives and lax.ppermute only.
A program may use at most 64 MiB of HBM per device.

v0:
```python
import jax
import jax.numpy as jnp
from jax import lax
from jax.sharding import PartitionSpec as P

WZ = 2
WH = 6
WW = 12
ZWIN = 2


epsilon = 1e-05


def from_behind(value, axis, by):
    devices = lax.axis_size(axis)
    return lax.ppermute(value, axis, [(i, (i + by) % devices) for i in range(devices)])


def allowed_pairs(level_win, lat_window, level_total, row_total):
    positions = jnp.arange(WZ * WH * WW, dtype=jnp.int32)
    level_pos = level_win * WZ + positions // (WH * WW)
    row_pos = lat_window * WH + positions // WW % WH
    labels = (level_pos >= level_total - WZ // 2).astype(jnp.int32) * 2 + (
        row_pos >= row_total - WH // 2
    ).astype(jnp.int32)
    return labels[:, None] == labels[None, :]


def to_windows(field):
    level_total, row_total, col_total, channels = field.shape
    blocks = field.reshape(
        level_total // WZ, WZ, row_total // WH, WH, col_total // WW, WW, channels
    )
    blocks = blocks.transpose(0, 2, 4, 1, 3, 5, 6)
    return blocks.reshape(
        level_total // WZ, row_total // WH, col_total // WW, WZ * WH * WW, channels
    )


def from_windows(blocks):
    level_win, lat_win, lon_win, token_count, channels = blocks.shape
    field = blocks.reshape(level_win, lat_win, lon_win, WZ, WH, WW, channels)
    field = field.transpose(0, 3, 1, 4, 2, 5, 6)
    return field.reshape(level_win * WZ, lat_win * WH, lon_win * WW, channels)


def band_backward(band_in, band_grad, gain, inproj_weight, outproj_weight, band_bias, allowed):
    window_count, token_count, channels = band_in.shape
    head_count = band_bias.shape[0]
    head_dim = channels // head_count
    scaling = head_dim ** (-0.5)
    floats = band_in.astype(jnp.float32)
    centred = floats - jnp.mean(floats, axis=-1, keepdims=True)
    inverse_rms = lax.rsqrt(jnp.mean(centred * centred, axis=-1, keepdims=True) + epsilon)
    standard = centred * inverse_rms
    normed = (standard * gain).astype(jnp.bfloat16)
    projected = jnp.dot(
        normed.reshape(-1, channels), inproj_weight, preferred_element_type=jnp.float32
    ).astype(jnp.bfloat16)
    projected = projected.reshape(window_count, token_count, 3, head_count, head_dim)
    query_rows = projected[:, :, 0]
    key_rows = projected[:, :, 1]
    value_rows = projected[:, :, 2]
    scores = (
        jnp.einsum("nihd,njhd->nhij", query_rows, key_rows, preferred_element_type=jnp.float32)
        * scaling
        + band_bias[None]
    )
    weights = jnp.where(allowed[None, None], jnp.exp(scores), 0.0)
    probabilities = weights / jnp.sum(weights, axis=-1, keepdims=True)
    upstream = lax.dot_general(
        band_grad.reshape(-1, channels),
        outproj_weight,
        (((1,), (1,)), ((), ())),
        preferred_element_type=jnp.float32,
    ).astype(jnp.bfloat16)
    upstream = upstream.reshape(window_count, token_count, head_count, head_dim)
    dprobs = jnp.einsum("nihd,njhd->nhij", upstream, value_rows, preferred_element_type=jnp.float32)
    inner_sum = jnp.sum(probabilities * dprobs, axis=-1, keepdims=True)
    dscores = probabilities * (dprobs - inner_sum)
    bias_part = jnp.sum(dscores, axis=0)
    probs_low = probabilities.astype(jnp.bfloat16)
    dscores_low = dscores.astype(jnp.bfloat16)
    dquery = (
        jnp.einsum("nhij,njhd->nihd", dscores_low, key_rows, preferred_element_type=jnp.float32)
        * scaling
    ).astype(jnp.bfloat16)
    dkeys = (
        jnp.einsum("nhij,nihd->njhd", dscores_low, query_rows, preferred_element_type=jnp.float32)
        * scaling
    ).astype(jnp.bfloat16)
    dvalues = jnp.einsum(
        "nhij,nihd->njhd", probs_low, upstream, preferred_element_type=jnp.float32
    ).astype(jnp.bfloat16)
    dprojected = jnp.stack([dquery, dkeys, dvalues], axis=2).reshape(-1, 3 * channels)
    dnormed = lax.dot_general(
        dprojected, inproj_weight, (((1,), (1,)), ((), ())), preferred_element_type=jnp.float32
    )
    dnormed = dnormed.reshape(window_count, token_count, channels)
    scaled = dnormed * gain
    grad_moved = inverse_rms * (
        scaled
        - jnp.mean(scaled, axis=-1, keepdims=True)
        - standard * jnp.mean(scaled * standard, axis=-1, keepdims=True)
    )
    return (grad_moved.astype(jnp.bfloat16), bias_part)


def moved_together(stacked):
    half_rows = WH // 2
    half_cols = WW // 2
    lon_count = lax.axis_size("lon")
    at_end = lax.axis_index("lon") == lon_count - 1
    inner = stacked[:, :, half_rows:, half_cols:]
    right = from_behind(stacked[:, :, half_rows:, :half_cols], "lon", -1)
    below = from_behind(stacked[:, :, :half_rows, half_cols:], "lat", -1)
    corner_piece = stacked[:, :, :half_rows, :half_cols]
    corner_far = from_behind(corner_piece, ("lat", "lon"), -(lon_count + 1))
    corner_near = from_behind(corner_piece, ("lat", "lon"), -1)
    corner = jnp.where(at_end, corner_near, corner_far)
    upper = jnp.concatenate([inner, right], axis=3)
    lower = jnp.concatenate([below, corner], axis=3)
    return jnp.concatenate([upper, lower], axis=2)


def returned_together(field_part):
    row_cut = field_part.shape[1] - WH // 2
    col_cut = field_part.shape[2] - WW // 2
    lon_count = lax.axis_size("lon")
    at_start = lax.axis_index("lon") == 0
    inner = field_part[:, :row_cut, :col_cut]
    below = from_behind(field_part[:, row_cut:, :col_cut], "lat", 1)
    right = from_behind(field_part[:, :row_cut, col_cut:], "lon", 1)
    corner_piece = field_part[:, row_cut:, col_cut:]
    corner_far = from_behind(corner_piece, ("lat", "lon"), lon_count + 1)
    corner_near = from_behind(corner_piece, ("lat", "lon"), 1)
    corner = jnp.where(at_start, corner_near, corner_far)
    upper = jnp.concatenate([corner, below], axis=2)
    lower = jnp.concatenate([right, inner], axis=2)
    return jnp.concatenate([upper, lower], axis=1)


def local(tokens, cotangent, norm_gain, inproj_weight, outproj_weight, bias):
    level_total = tokens.shape[0]
    row_total = tokens.shape[1] * lax.axis_size("lat")
    lat_local = tokens.shape[1] // WH
    stacked = jnp.stack([tokens, cotangent])
    moved = moved_together(stacked)
    moved = jnp.roll(moved, -(WZ // 2), axis=1)
    in_windows = to_windows(moved[0])
    grad_windows = to_windows(moved[1])
    lat_windows = lax.axis_index("lat") * lat_local + jnp.arange(lat_local, dtype=jnp.int32)
    grad_levels = []
    bias_levels = []
    for level_win in range(ZWIN):

        def one_band(operands, level_win=level_win):
            band_in, band_grad, band_bias, lat_window = operands
            allowed = allowed_pairs(level_win, lat_window, level_total, row_total)
            return band_backward(
                band_in, band_grad, norm_gain, inproj_weight, outproj_weight, band_bias, allowed
            )

        grad_blocks, bias_parts = lax.map(
            one_band, (in_windows[level_win], grad_windows[level_win], bias[level_win], lat_windows)
        )
        grad_levels.append(grad_blocks)
        bias_levels.append(bias_parts)
    bias_local = jnp.stack(bias_levels)
    bias_local = lax.psum_scatter(
        bias_local.astype(jnp.bfloat16), "lon", scatter_dimension=3, tiled=True
    ).astype(jnp.float32)
    grad_field = from_windows(jnp.stack(grad_levels))
    grad_field = jnp.roll(grad_field, WZ // 2, axis=0)
    grad_input = returned_together(grad_field)
    return (grad_input, bias_local)


def solution(mesh):
    placed = (
        P(None, "lat", "lon", None),
        P(None, "lat", "lon", None),
        P(),
        P(),
        P(),
        P(None, "lat", None, None, None),
    )
    return jax.shard_map(
        local,
        mesh=mesh,
        in_specs=placed,
        out_specs=(P(None, "lat", "lon", None), P(None, "lat", None, "lon", None)),
        check_vma=False,
    )
```

profile of v0, /device:TPU:0, one launch (start us, length us, event | category | flops | bytes accessed | tf_op | source)
XLA Modules:
  0.0 94.7 jit_solution(3000681755455278250)
XLA Ops:
  7.2 1.0 %fusion.43 = (bf16[2,4,3,6,192]{4,3,2,1,0:T(8,128)(2,1)S(1)}, bf16[2,4,3,6,192]{4,3,2,1,0:T(8,128)(2,1)S(1)}) fusion(bf16[1,4,6,24,192]{4,3,2,1,0:T(8,128)(2,1)} %bitcast.130, bf16[1,4,6,24,192]{4,3,2,1,0:T(8,128)(2,1)} %bitcast.132), kind=kLoop, calls=%fused_computation.101 | loop fusion | flops 221184 | bytes 552960 | tf_op jit(solution)/shard_map/stack | solution.py:148
  8.3 6.4 %collective-permute-start.2 = (bf16[2,4,3,6,192]{4,3,2,1,0:T(8,128)(2,1)S(1)}, bf16[2,4,3,6,192]{4,3,2,1,0:T(8,128)(2,1)S(1)}, u32[]{:S(2)}, u32[]{:S(2)}) collective-permute-start(bf16[2,4,3,6,192]{4,3,2,1,0:T(8,128)(2,1)S(1)} %get-tuple-element.91), channel_id=1, source_target_pairs={{0,31},{1,0},{2,1},{3,2},{4,3},{5,4},{6,5},{7,6},{8,7},{9,8},{10,9... | collective-permute-start | bytes 165896 | tf_op jit(solution)/shard_map/ppermute | solution.py:17
  14.7 1.1 %collective-permute-start.3 = (bf16[2,4,3,6,192]{4,3,2,1,0:T(8,128)(2,1)S(1)}, bf16[2,4,3,6,192]{4,3,2,1,0:T(8,128)(2,1)S(1)}, u32[]{:S(2)}, u32[]{:S(2)}) collective-permute-start(bf16[2,4,3,6,192]{4,3,2,1,0:T(8,128)(2,1)S(1)} %get-tuple-element.91), channel_id=1, source_target_pairs={{0,27},{1,28},{2,29},{3,30},{4,31},{5,0},{6,1},{7,2},{8,3},{9,4},{... | collective-permute-start | bytes 165896 | tf_op jit(solution)/shard_map/ppermute | solution.py:17
  15.8 1.3 %fusion.23 = (bf16[2,4,3,18,192]{4,3,2,1,0:T(8,128)(2,1)S(1)}, bf16[2,4,3,18,192]{4,3,2,1,0:T(8,128)(2,1)S(1)}) fusion(bf16[1,4,6,24,192]{4,3,2,1,0:T(8,128)(2,1)} %bitcast.131, bf16[1,4,6,24,192]{4,3,2,1,0:T(8,128)(2,1)} %bitcast.133), kind=kLoop, calls=%fused_computation.59 | loop fusion | flops 165888 | bytes 774144 | tf_op jit(solution)/shard_map/stack | solution.py:148
  17.2 1.7 %collective-permute-start = (bf16[2,4,3,6,192]{4,3,2,1,0:T(8,128)(2,1)S(1)}, bf16[2,4,3,6,192]{4,3,2,1,0:T(8,128)(2,1)S(1)}, u32[]{:S(2)}, u32[]{:S(2)}) collective-permute-start(bf16[2,4,3,6,192]{4,3,2,1,0:T(8,128)(2,1)S(1)} %get-tuple-element.90), channel_id=1, source_target_pairs={{0,3},{1,0},{2,1},{3,2},{4,7},{5,4},{6,5},{7,6},{8,11},{9,8},{10,9... | collective-permute-start | bytes 165896 | tf_op jit(solution)/shard_map/ppermute | solution.py:17
  19.1 0.7 broadcast_compare_fusion
  19.8 0.7 broadcast_compare_fusion.1
  20.5 1.4 %copy.157 = f32[6,144,144]{1,2,0:T(8,128)} copy(f32[6,144,144]{2,1,0:T(8,128)S(1)} %get-tuple-element.69) | data formatting | bytes 995328 | tf_op jit(solution)/shard_map/while/body/eval_jaxpr/add | solution.py:66
  21.8 1.3 %copy.131 = f32[6,144,144]{1,2,0:T(8,128)} copy(f32[6,144,144]{2,1,0:T(8,128)S(1)} %get-tuple-element.68) | data formatting | bytes 995328 | tf_op jit(solution)/shard_map/while/body/eval_jaxpr/add | solution.py:66
  24.1 0.2 fusion.45
  24.3 0.6 multiply_reduce_fusion.5
  25.0 0.5 multiply_reduce_fusion.3
  26.7 0.3 convolution_convert_fusion
  27.1 0.2 copy.154
  27.5 1.2 %fusion.55 = (bf16[2,144,1,6,32]{1,0,4,3,2:T(2,128)(2,1)}, bf16[2,144,1,6,32]{1,0,4,3,2:T(2,128)(2,1)}, bf16[2,144,1,6,32]{1,0,4,3,2:T(2,128)(2,1)}) fusion(bf16[2,144,3,6,32]{1,0,4,3,2:T(2,128)(2,1)S(1)} %reshape.364), kind=kLoop, calls=%fused_computation.138 | loop fusion | bytes 663552 | tf_op jit(solution)/shard_map/while/body/eval_jaxpr/slice | solution.py:64
  29.1 0.9 fusion.57
  30.6 1.4 %fusion.30 = f32[2,6,144,144]{2,3,1,0:T(8,128)S(1)} fusion(bf16[2,144,1,6,32]{1,0,4,3,2:T(2,128)(2,1)} %get-tuple-element.83, bf16[2,144,6,32]{1,0,3,2:T(2,128)(2,1)S(1)} %reshape.366), kind=kOutput, calls=%fused_computation.81 | convolution fusion | flops 15925248 | bytes 1216512 | tf_op jit(solution)/shard_map/while/body/eval_jaxpr/nihd,njhd->nhij/dot_general | solution.py:79
  32.0 3.9 %multiply_reduce_fusion = (f32[2,6,144]{2,1,0:T(8,128)}, f32[2,6,144,144]{2,3,1,0:T(8,128)}) fusion(f32[2,6,144,144]{2,3,1,0:T(8,128)S(1)} %fusion.30, f32[6,144,144]{1,2,0:T(8,128)} %copy.157, pred[144,144]{0,1:T(8,128)(4,1)} %broadcast_compare_fusion, bf16[2,144,1,6,32]{1,0,4,3,2:T(2,128)(2,1)S(1)} %copy-done.7, bf16[2,144,1,6,32]{1,0,4,3,2:T(2,128)(2,1)S(1)} %copy-done.9), kind=kOutput, calls=%fused_computation.1 | convolution fusion | flops 17418384 | bytes 2737152 | tf_op jit(solution)/shard_map/while/body/eval_jaxpr/div | solution.py:71
  35.9 2.7 %fusion.5 = bf16[2,144,1,6,32]{1,4,3,0,2:T(8,128)(2,1)} fusion(f32[2,6,144,144]{2,3,1,0:T(8,128)} %get-tuple-element.99, bf16[2,144,6,32]{1,0,3,2:T(2,128)(2,1)S(1)} %reshape.366), kind=kOutput, calls=%fused_computation.23 | convolution fusion | flops 16229376 | bytes 1216512 | tf_op jit(solution)/shard_map/while/body/eval_jaxpr/nhij,nihd->njhd/dot_general | solution.py:93
  38.6 0.5 fusion.18
  39.1 0.4 copy-done.10
  39.5 1.1 %fusion.6 = bf16[2,144,1,6,32]{1,4,3,0,2:T(8,128)(2,1)} fusion(bf16[2,6,144,144]{2,3,1,0:T(8,128)(2,1)S(1)} %get-tuple-element.67, bf16[2,144,1,6,32]{1,0,4,3,2:T(2,128)(2,1)S(1)} %copy-done.10), kind=kOutput, calls=%fused_computation.24 | convolution fusion | flops 16035840 | bytes 718848 | tf_op jit(solution)/shard_map/while/body/eval_jaxpr/nhij,nihd->njhd/dot_general | solution.py:90
  40.6 1.0 %fusion.7 = bf16[2,144,1,6,32]{1,4,3,0,2:T(8,128)(2,1)} fusion(bf16[2,6,144,144]{2,3,1,0:T(8,128)(2,1)S(1)} %get-tuple-element.67, bf16[2,144,1,6,32]{1,0,4,3,2:T(2,128)(2,1)S(1)} %copy-done.8), kind=kOutput, calls=%fused_computation.25 | convolution fusion | flops 16035840 | bytes 718848 | tf_op jit(solution)/shard_map/while/body/eval_jaxpr/nhij,njhd->nihd/dot_general | solution.py:86
  42.5 0.3 convolution_convert_fusion.1
  42.9 0.2 copy.128
  43.4 1.3 %fusion.54 = (bf16[2,144,1,6,32]{1,0,4,3,2:T(2,128)(2,1)}, bf16[2,144,1,6,32]{1,0,4,3,2:T(2,128)(2,1)}, bf16[2,144,1,6,32]{1,0,4,3,2:T(2,128)(2,1)S(1)}) fusion(bf16[2,144,3,6,32]{1,0,4,3,2:T(2,128)(2,1)S(1)} %reshape.361), kind=kLoop, calls=%fused_computation.137 | loop fusion | bytes 663552 | tf_op jit(solution)/shard_map/while/body/eval_jaxpr/slice | solution.py:64
  45.3 1.4 %fusion.31 = f32[2,6,144,144]{2,3,1,0:T(8,128)S(1)} fusion(bf16[2,144,1,6,32]{1,0,4,3,2:T(2,128)(2,1)} %get-tuple-element.80, bf16[2,144,6,32]{1,0,3,2:T(2,128)(2,1)S(1)} %reshape.363), kind=kOutput, calls=%fused_computation.85 | convolution fusion | flops 15925248 | bytes 1216512 | tf_op jit(solution)/shard_map/while/body/eval_jaxpr/nihd,njhd->nhij/dot_general | solution.py:79
  46.6 3.4 %multiply_reduce_fusion.1 = (f32[2,6,144]{2,1,0:T(8,128)S(1)}, f32[2,6,144,144]{2,3,1,0:T(8,128)}) fusion(f32[2,6,144,144]{2,3,1,0:T(8,128)S(1)} %fusion.31, f32[6,144,144]{1,2,0:T(8,128)} %copy.131, pred[144,144]{0,1:T(8,128)(4,1)S(1)} %copy-done.15, bf16[2,144,1,6,32]{1,0,4,3,2:T(2,128)(2,1)S(1)} %get-tuple-element.82, ...), kind=kOutput, calls=%fused_computation.4 | convolution fusion | flops 17418384 | bytes 2737152 | tf_op jit(solution)/shard_map/while/body/eval_jaxpr/div | solution.py:71
  50.1 2.0 %fusion.4 = bf16[2,144,1,6,32]{1,4,3,0,2:T(8,128)(2,1)S(1)} fusion(f32[2,6,144,144]{2,3,1,0:T(8,128)} %get-tuple-element.102, bf16[2,144,6,32]{1,0,3,2:T(2,128)(2,1)S(1)} %reshape.363), kind=kOutput, calls=%fused_computation.22 | convolution fusion | flops 16229376 | bytes 1216512 | tf_op jit(solution)/shard_map/while/body/eval_jaxpr/nhij,nihd->njhd/dot_general | solution.py:93
  52.1 0.5 fusion.16
  52.6 0.4 copy-done.11
  53.0 0.4 fusion.8
  53.4 0.4 fusion.9
  54.0 0.6 fusion.53
  54.9 0.6 fusion.52
  55.7 2.0 %copy.173 = bf16[2,1,6,144,144]{4,2,1,0,3:T(8,128)(2,1)} copy(bf16[2,1,6,144,144]{3,4,2,1,0:T(8,128)(2,1)S(1)} %pad_maximum_fusion) | data formatting | bytes 995328 | tf_op jit(solution)/shard_map/stack | solution.py:170
  58.4 0.5 maximum_bitcast_fusion
  59.1 0.3 reshape.367
  59.7 1.4 %collective-permute-start.4 = (bf16[4,3,6,192]{3,0,2,1:T(4,128)(2,1)S(1)}, bf16[4,3,6,192]{3,0,2,1:T(4,128)(2,1)S(1)}, u32[]{:S(2)}, u32[]{:S(2)}) collective-permute-start(bf16[4,3,6,192]{3,0,2,1:T(4,128)(2,1)S(1)} %get-tuple-element.92), channel_id=1, source_target_pairs={{0,1},{1,2},{2,3},{3,4},{4,5},{5,6},{6,7},{7,8},{8,9},{9,10},{10,1... | collective-permute-start | bytes 82952 | tf_op jit(solution)/shard_map/ppermute | solution.py:17
  61.0 0.7 collective-permute-start.5
  61.8 0.6 collective-permute-start.7
  62.4 1.0 %collective-permute-start.6 = (bf16[4,3,18,192]{3,0,2,1:T(4,128)(2,1)S(1)}, bf16[4,3,18,192]{3,0,2,1:T(4,128)(2,1)S(1)}, u32[]{:S(2)}, u32[]{:S(2)}) collective-permute-start(bf16[4,3,18,192]{3,0,2,1:T(4,128)(2,1)S(1)} %fusion.42), channel_id=1, source_target_pairs={{0,4},{4,8},{8,12},{12,16},{16,20},{20,24},{24,28},{28,0},{1,5},{5... | collective-permute-start | bytes 248840 | tf_op jit(solution)/shard_map/ppermute | solution.py:17
  63.4 3.4 %collective-permute-done.4 = bf16[4,3,6,192]{3,0,2,1:T(4,128)(2,1)S(1)} collective-permute-done((bf16[4,3,6,192]{3,0,2,1:T(4,128)(2,1)S(1)}, bf16[4,3,6,192]{3,0,2,1:T(4,128)(2,1)S(1)}, u32[]{:S(2)}, u32[]{:S(2)}) %collective-permute-start.4) | collective-permute-done | bytes 27680 | tf_op jit(solution)/shard_map/ppermute | solution.py:17
  66.8 1.9 %collective-permute-done.5 = bf16[4,3,6,192]{3,0,2,1:T(4,128)(2,1)S(1)} collective-permute-done((bf16[4,3,6,192]{3,0,2,1:T(4,128)(2,1)S(1)}, bf16[4,3,6,192]{3,0,2,1:T(4,128)(2,1)S(1)}, u32[]{:S(2)}, u32[]{:S(2)}) %collective-permute-start.5) | collective-permute-done | bytes 27680 | tf_op jit(solution)/shard_map/ppermute | solution.py:17
  68.7 0.3 collective-permute-done.7
  69.2 0.7 copy.174
  70.0 15.8 %reduce-scatter.2.cloned.1.call-done = bf16[2,1,6,36,144]{4,2,1,0,3:T(8,128)(2,1)} async-done(((bf16[2,1,6,144,144]{4,2,1,0,3:T(8,128)(2,1)}), bf16[2,1,6,36,144]{4,2,1,0,3:T(8,128)(2,1)}) %reduce-scatter.2.cloned.1.call-update) | async-done | bytes 124432 | tf_op jit(solution)/shard_map/reduce_scatter | solution.py:171
  85.8 2.1 %copy.175 = f32[2,1,6,36,144]{4,1,3,2,0:T(1,128)} copy(bf16[2,1,6,36,144]{4,2,1,0,3:T(8,128)(2,1)} %reduce-scatter.2.cloned.1.call-done) | data formatting | bytes 373248
  (106 shorter events, 7.4 us)
Async XLA Ops:
  7.2 19.5 %copy-start = (bf16[192,576]{1,0:T(8,128)(2,1)S(1)}, bf16[192,576]{1,0:T(8,128)(2,1)}, u32[]{:S(2)}) copy-start(bf16[192,576]{1,0:T(8,128)(2,1)} %param.9) | copy-start | bytes 663556
  7.2 78.6 %reduce-scatter.2.cloned.1.call-start = ((), (), s32[]{:S(2)}) async-start(), calls=%async_computation.1 | async-start | bytes 1474560 | tf_op jit(solution)/shard_map/reduce_scatter | solution.py:171
  7.2 11.7 %copy-start.3 = (f32[2,1,6,144,144]{4,3,2,1,0:T(8,128)S(1)}, f32[2,1,6,144,144]{4,3,2,1,0:T(8,128)}, u32[]{:S(2)}) copy-start(f32[2,1,6,144,144]{4,3,2,1,0:T(8,128)} %param.11) | copy-start | bytes 2985988
  8.3 14.9 %collective-permute-start.2 = (bf16[2,4,3,6,192]{4,3,2,1,0:T(8,128)(2,1)S(1)}, bf16[2,4,3,6,192]{4,3,2,1,0:T(8,128)(2,1)S(1)}, u32[]{:S(2)}, u32[]{:S(2)}) collective-permute-start(bf16[2,4,3,6,192]{4,3,2,1,0:T(8,128)(2,1)S(1)} %get-tuple-element.91), channel_id=1, source_target_pairs={{0,31},{1,0},{2,1},{3,2},{4,3},{5,4},{6,5},{7,6},{8,7},{9,8},{10,9... | collective-permute-start | bytes 165896 | tf_op jit(solution)/shard_map/ppermute | solution.py:17
  14.7 8.5 %collective-permute-start.3 = (bf16[2,4,3,6,192]{4,3,2,1,0:T(8,128)(2,1)S(1)}, bf16[2,4,3,6,192]{4,3,2,1,0:T(8,128)(2,1)S(1)}, u32[]{:S(2)}, u32[]{:S(2)}) collective-permute-start(bf16[2,4,3,6,192]{4,3,2,1,0:T(8,128)(2,1)S(1)} %get-tuple-element.91), channel_id=1, source_target_pairs={{0,27},{1,28},{2,29},{3,30},{4,31},{5,0},{6,1},{7,2},{8,3},{9,4},{... | collective-permute-start | bytes 165896 | tf_op jit(solution)/shard_map/ppermute | solution.py:17
  17.1 6.1 %collective-permute-start.1 = (bf16[2,4,3,18,192]{4,3,2,1,0:T(8,128)(2,1)S(1)}, bf16[2,4,3,18,192]{4,3,2,1,0:T(8,128)(2,1)S(1)}, u32[]{:S(2)}, u32[]{:S(2)}) collective-permute-start(bf16[2,4,3,18,192]{4,3,2,1,0:T(8,128)(2,1)S(1)} %get-tuple-element.89), channel_id=1, source_target_pairs={{0,28},{4,0},{8,4},{12,8},{16,12},{20,16},{24,20},{28,24},{1,29},{... | collective-permute-start | bytes 497672 | tf_op jit(solution)/shard_map/ppermute | solution.py:17
  17.2 6.0 %collective-permute-start = (bf16[2,4,3,6,192]{4,3,2,1,0:T(8,128)(2,1)S(1)}, bf16[2,4,3,6,192]{4,3,2,1,0:T(8,128)(2,1)S(1)}, u32[]{:S(2)}, u32[]{:S(2)}) collective-permute-start(bf16[2,4,3,6,192]{4,3,2,1,0:T(8,128)(2,1)S(1)} %get-tuple-element.90), channel_id=1, source_target_pairs={{0,3},{1,0},{2,1},{3,2},{4,7},{5,4},{6,5},{7,6},{8,11},{9,8},{10,9... | collective-permute-start | bytes 165896 | tf_op jit(solution)/shard_map/ppermute | solution.py:17
  25.0 1.7 %copy-start.17 = (f32[192]{0:T(256)S(1)}, f32[192]{0:T(256)}, u32[]{:S(2)}) copy-start(f32[192]{0:T(256)} %param.8) | copy-start | bytes 2308
  27.5 2.6 %copy-start.13 = (bf16[192,192]{1,0:T(8,128)(2,1)S(1)}, bf16[192,192]{1,0:T(8,128)(2,1)}, u32[]{:S(2)}) copy-start(bf16[192,192]{1,0:T(8,128)(2,1)} %param.10) | copy-start | bytes 221188
  30.0 2.0 %copy-start.7 = (bf16[2,144,1,6,32]{1,0,4,3,2:T(2,128)(2,1)S(1)}, bf16[2,144,1,6,32]{1,0,4,3,2:T(2,128)(2,1)}, u32[]{:S(2)}) copy-start(bf16[2,144,1,6,32]{1,0,4,3,2:T(2,128)(2,1)} %get-tuple-element.85) | copy-start | bytes 331780
  30.0 2.0 %copy-start.9 = (bf16[2,144,1,6,32]{1,0,4,3,2:T(2,128)(2,1)S(1)}, bf16[2,144,1,6,32]{1,0,4,3,2:T(2,128)(2,1)}, u32[]{:S(2)}) copy-start(bf16[2,144,1,6,32]{1,0,4,3,2:T(2,128)(2,1)} %get-tuple-element.84) | copy-start | bytes 331780
  35.9 2.7 %copy-start.1 = (f32[2,6,144,144]{2,3,1,0:T(8,128)S(1)}, f32[2,6,144,144]{2,3,1,0:T(8,128)}, u32[]{:S(2)}) copy-start(f32[2,6,144,144]{2,3,1,0:T(8,128)} %get-tuple-element.99) | copy-start | bytes 2985988
  35.9 2.7 %copy-start.16 = (f32[2,6,144]{2,1,0:T(8,128)S(1)}, f32[2,6,144]{2,1,0:T(8,128)}, u32[]{:S(2)}) copy-start(f32[2,6,144]{2,1,0:T(8,128)} %get-tuple-element.98) | copy-start | bytes 20740
  38.6 0.9 copy-start.10
  38.6 2.0 %copy-start.8 = (bf16[2,144,1,6,32]{1,0,4,3,2:T(2,128)(2,1)S(1)}, bf16[2,144,1,6,32]{1,0,4,3,2:T(2,128)(2,1)}, u32[]{:S(2)}) copy-start(bf16[2,144,1,6,32]{1,0,4,3,2:T(2,128)(2,1)} %get-tuple-element.85) | copy-start | bytes 331780
  42.5 2.1 %copy-start.12 = (bf16[1,1,2,2,6,12,192]{6,3,0,5,2,4,1:T(2,128)(2,1)S(1)}, bf16[1,1,2,2,6,12,192]{6,3,0,5,2,4,1:T(2,128)(2,1)}, u32[]{:S(2)}) copy-start(bf16[1,1,2,2,6,12,192]{6,3,0,5,2,4,1:T(2,128)(2,1)} %get-tuple-element.94) | copy-start | bytes 331780
  42.9 1.9 %copy-start.14 = (bf16[192,192]{1,0:T(8,128)(2,1)S(1)}, bf16[192,192]{1,0:T(8,128)(2,1)}, u32[]{:S(2)}) copy-start(bf16[192,192]{1,0:T(8,128)(2,1)} %param.10) | copy-start | bytes 221188
  44.7 2.0 %copy-start.15 = (pred[144,144]{0,1:T(8,128)(4,1)S(1)}, pred[144,144]{0,1:T(8,128)(4,1)}, u32[]{:S(2)}) copy-start(pred[144,144]{0,1:T(8,128)(4,1)} %broadcast_compare_fusion.1) | copy-start | bytes 62212
  50.1 2.0 %copy-start.2 = (f32[2,6,144,144]{2,3,1,0:T(8,128)S(1)}, f32[2,6,144,144]{2,3,1,0:T(8,128)}, u32[]{:S(2)}) copy-start(f32[2,6,144,144]{2,3,1,0:T(8,128)} %get-tuple-element.102) | copy-start | bytes 2985988
  52.1 0.9 copy-start.11
  52.5 1.3 %copy-start.4 = (bf16[2,144,1,6,32]{1,4,3,0,2:T(8,128)(2,1)S(1)}, bf16[2,144,1,6,32]{1,4,3,0,2:T(8,128)(2,1)}, u32[]{:S(2)}) copy-start(bf16[2,144,1,6,32]{1,4,3,0,2:T(8,128)(2,1)} %fusion.5) | copy-start | bytes 331780
  52.6 1.3 %copy-start.5 = (bf16[2,144,1,6,32]{1,4,3,0,2:T(8,128)(2,1)S(1)}, bf16[2,144,1,6,32]{1,4,3,0,2:T(8,128)(2,1)}, u32[]{:S(2)}) copy-start(bf16[2,144,1,6,32]{1,4,3,0,2:T(8,128)(2,1)} %fusion.6) | copy-start | bytes 331780
  52.6 1.3 %copy-start.6 = (bf16[2,144,1,6,32]{1,4,3,0,2:T(8,128)(2,1)S(1)}, bf16[2,144,1,6,32]{1,4,3,0,2:T(8,128)(2,1)}, u32[]{:S(2)}) copy-start(bf16[2,144,1,6,32]{1,4,3,0,2:T(8,128)(2,1)} %fusion.7) | copy-start | bytes 331780
  59.7 7.2 %collective-permute-start.4 = (bf16[4,3,6,192]{3,0,2,1:T(4,128)(2,1)S(1)}, bf16[4,3,6,192]{3,0,2,1:T(4,128)(2,1)S(1)}, u32[]{:S(2)}, u32[]{:S(2)}) collective-permute-start(bf16[4,3,6,192]{3,0,2,1:T(4,128)(2,1)S(1)} %get-tuple-element.92), channel_id=1, source_target_pairs={{0,1},{1,2},{2,3},{3,4},{4,5},{5,6},{6,7},{7,8},{8,9},{9,10},{10,1... | collective-permute-start | bytes 82952 | tf_op jit(solution)/shard_map/ppermute | solution.py:17
  61.0 7.7 %collective-permute-start.5 = (bf16[4,3,6,192]{3,0,2,1:T(4,128)(2,1)S(1)}, bf16[4,3,6,192]{3,0,2,1:T(4,128)(2,1)S(1)}, u32[]{:S(2)}, u32[]{:S(2)}) collective-permute-start(bf16[4,3,6,192]{3,0,2,1:T(4,128)(2,1)S(1)} %get-tuple-element.92), channel_id=1, source_target_pairs={{0,5},{1,6},{2,7},{3,8},{4,9},{5,10},{6,11},{7,12},{8,13},{9,14},{... | collective-permute-start | bytes 82952 | tf_op jit(solution)/shard_map/ppermute | solution.py:17
  61.8 7.1 %collective-permute-start.7 = (bf16[4,3,6,192]{3,0,2,1:T(4,128)(2,1)S(1)}, bf16[4,3,6,192]{3,0,2,1:T(4,128)(2,1)S(1)}, u32[]{:S(2)}, u32[]{:S(2)}) collective-permute-start(bf16[4,3,6,192]{3,0,2,1:T(4,128)(2,1)S(1)} %get-tuple-element.93), channel_id=1, source_target_pairs={{0,1},{1,2},{2,3},{3,0},{4,5},{5,6},{6,7},{7,4},{8,9},{9,10},{10,1... | collective-permute-start | bytes 82952 | tf_op jit(solution)/shard_map/ppermute | solution.py:17
  62.4 6.6 %collective-permute-start.6 = (bf16[4,3,18,192]{3,0,2,1:T(4,128)(2,1)S(1)}, bf16[4,3,18,192]{3,0,2,1:T(4,128)(2,1)S(1)}, u32[]{:S(2)}, u32[]{:S(2)}) collective-permute-start(bf16[4,3,18,192]{3,0,2,1:T(4,128)(2,1)S(1)} %fusion.42), channel_id=1, source_target_pairs={{0,4},{4,8},{8,12},{12,16},{16,20},{20,24},{24,28},{28,0},{1,5},{5... | collective-permute-start | bytes 248840 | tf_op jit(solution)/shard_map/ppermute | solution.py:17
Sparse Core Ops, SparseCore 0:
  57.8 27.9 reduce-scatter.1
where the time goes:
time: 95 us; the launch traced here: 94.7 us
  waiting for transfers between devices  21.4 us (23%)
  matrix products  19.9 us (21%)
  local copies, waits for them, and re-layouts  17.3 us (18%)
  between operations  14.7 us (15%)
  starting transfers between devices  12.9 us (14%)
  other arithmetic  8.53 us (9%)
    reduce_scatter x1, waiting for transfers between devices, local(): lax.psum_scatter(bias_local.astype(jnp.bfloat16), 'lon', scatter_dimensio...  15.8 us
    ppermute x8, starting transfers between devices, from_behind(): lax.ppermute(value, axis, [(i, (i + by) % devices) for i in range(devices)])  12.9 us
    div x2, matrix products, band_backward(): probabilities = weights / jnp.sum(weights, axis=-1, keepdims=True)  7.31 us
    ppermute x8, waiting for transfers between devices, from_behind(): lax.ppermute(value, axis, [(i, (i + by) % devices) for i in range(devices)])  5.57 us
    dot_general x2, matrix products, band_backward(): jnp.einsum('nhij,nihd->njhd', probs_low, upstream, preferred_element_type...  4.65 us
    unnamed x38, local copies, waits for them, and re-layouts  3.77 us
    add x3, local copies, waits for them, and re-layouts, band_backward(): jnp.einsum('nihd,njhd->nhij', query_rows, key_rows, preferred_element_typ...  2.83 us
    dot_general x2, matrix products, band_backward(): jnp.einsum('nihd,njhd->nhij', upstream, value_rows, preferred_element_typ...  2.74 us
  transfers between devices with their start and end apart: 9, of which 4 were waited for; matrix products, arithmetic and copies ran while one was open for 9% of the time, Pallas kernels for 0%

commit v1 on v0

v1 whole, which is shorter than its diff:
```python
import functools

import jax
import jax.numpy as jnp
import numpy as np
from jax import lax
from jax.experimental import pallas as pl
from jax.experimental.pallas import tpu as pltpu
from jax.sharding import PartitionSpec as P

WZ = 2
WH = 6
WW = 12
WT = WZ * WH * WW
HALF_ROWS = WH // 2
HALF_COLS = WW // 2
SIDE = 8
LEVEL = WH * WW
MAIN = 128
REM = WT - MAIN
LOG2E = 1.4426950408889634
epsilon = 1e-05
F32 = jnp.float32
BF16 = jnp.bfloat16
NT = (((1,), (1,)), ((), ()))


def dot(a, b):
    return jnp.dot(a, b, preferred_element_type=F32)


def dot_nt(a, b):
    return lax.dot_general(a, b, NT, preferred_element_type=F32)


def round_up(value, to):
    return (value + to - 1) // to * to


def window_order(cols):
    windows = cols // WW
    part = HALF_ROWS * cols
    side = HALF_ROWS * SIDE
    table = np.zeros((windows * LEVEL, 2 * part + 2 * side), np.float32)
    for c in range(windows):
        for r in range(WH):
            for w in range(WW):
                col = c * WW + w + HALF_COLS
                low, row = divmod(r, HALF_ROWS)
                if col < cols:
                    at = low * part + row * cols + col
                else:
                    at = 2 * part + low * side + row * SIDE + col - cols
                table[c * LEVEL + r * WW + w, at] = 1.0
    return table


def query_choice(parts, heads):
    chunk = WT // parts
    table = np.zeros((parts, round_up(chunk, 16), MAIN + heads * REM), np.float32)
    for j in range(parts):
        for i in range(chunk):
            query = j * chunk + i
            if query < MAIN:
                table[j, i, query] = 1.0
            else:
                table[j, i, MAIN + query - MAIN :: REM] = 1.0
    return table


def send_kernel(tok, cot, below, right, corner):
    levels = tok.shape[0]
    for which, src in enumerate((tok, cot)):
        for level in range(levels):
            to = which * levels + level
            for row in range(HALF_ROWS):
                upper = src[level, row]
                below[to, row] = upper
                corner[to, row] = upper[:SIDE]
                right[to, row] = src[level, HALF_ROWS + row][:SIDE]


def prep_kernel(heads, lat_count, bias, inproj, bias_t, weights):
    channels = inproj.shape[0]
    level_windows = bias.shape[0]
    for part in range(3):
        weights[part] = inproj[:, part * channels : (part + 1) * channels]
    last_lat = lax.axis_index("lat") == lat_count - 1

    def labels(index, window):
        level_label = (index >= LEVEL) & (window == level_windows - 1)
        in_level = jnp.where(index >= LEVEL, index - LEVEL, index)
        row_label = (in_level >= LEVEL // 2) & last_lat
        return level_label.astype(jnp.int32) * 2 + row_label.astype(jnp.int32)

    for window in range(level_windows):
        key_index = lax.broadcasted_iota(jnp.int32, (WT, MAIN), 0)
        query_index = lax.broadcasted_iota(jnp.int32, (WT, MAIN), 1)
        allowed = labels(key_index, window) == labels(query_index, window)
        for head in range(heads):
            piece = jnp.transpose(bias[window, head, :MAIN, :]) * LOG2E
            bias_t[window, :, head * MAIN : (head + 1) * MAIN] = jnp.where(allowed, piece, -1e30)
        key_index = lax.broadcasted_iota(jnp.int32, (WT, heads * REM), 0)
        allowed = labels(key_index, window) == labels(jnp.full_like(key_index, WT - 1), window)
        rest = jnp.concatenate([bias[window, head, MAIN:, :] for head in range(heads)], axis=0)
        bias_t[window, :, heads * MAIN :] = jnp.where(allowed, jnp.transpose(rest) * LOG2E, -1e30)


def layer_kernel(
    heads, parts, tok, cot, below, right, corner, gain_ref, weights, outproj, bias_t, perm, perm_t, choice,
    g_inner, g_below, g_right, g_corner, *rest,
):
    chunks, bias_acc = rest[:-1], rest[-1]
    levels, _, cols, channels = tok.shape
    head_dim = channels // heads
    scaling = head_dim ** (-0.5)
    level_windows = levels // WZ
    lon_windows = cols // WW
    chunk = WT // parts
    wide = choice.shape[1]
    gain = gain_ref[...]
    wq, wk, wv = weights[0], weights[1], weights[2]
    out_w = outproj[...]
    lane_head = lax.broadcasted_iota(jnp.int32, (1, channels), 1) // head_dim
    head_masks = [(lane_head == head).astype(F32).astype(BF16) for head in range(heads)]
    rest_lane = lax.broadcasted_iota(jnp.int32, (1, heads * REM), 1) // REM
    rest_masks = [(rest_lane == head).astype(F32).astype(BF16) for head in range(heads)]
    me = lax.axis_index("lon")
    picks = jnp.concatenate(
        [choice[lax.rem(me + d, parts)] for d in range(parts)], axis=0
    )

    def gathered(source, offset, level):
        rows = [source[level, HALF_ROWS + row] for row in range(HALF_ROWS)]
        for piece in (below, right, corner):
            rows += [piece[offset + level, row] for row in range(HALF_ROWS)]
        stacked = jnp.concatenate([row.astype(F32) for row in rows], axis=0).astype(BF16)
        return dot(perm[...], stacked)

    def stack_heads(value):
        main = [value[:MAIN] * mask for mask in head_masks]
        left = [value[MAIN:] * mask for mask in head_masks]
        return jnp.concatenate(main + left, axis=0)

    def level_window(window, _):
        at = [lax.rem(window * WZ + WZ // 2 + li, levels) for li in range(WZ)]
        t_parts = [gathered(tok, 0, level) for level in at]
        g_parts = [gathered(cot, levels, level) for level in at]
        grads = []
        for c in range(lon_windows):
            cut = slice(c * LEVEL, (c + 1) * LEVEL)
            t = jnp.concatenate([part[cut] for part in t_parts], axis=0)
            g = jnp.concatenate([part[cut] for part in g_parts], axis=0).astype(BF16)
            centred = t - jnp.mean(t, axis=-1, keepdims=True)
            inverse_rms = lax.rsqrt(jnp.mean(centred * centred, axis=-1, keepdims=True) + epsilon)
            standard = centred * inverse_rms
            normed = (standard * gain).astype(BF16)
            q = dot(normed, wq).astype(BF16)
            k32 = dot(normed, wk)
            k = k32.astype(BF16)
            k_t = jnp.transpose(k32).astype(BF16)
            v = dot(normed, wv).astype(BF16)
            u = dot_nt(g, out_w).astype(BF16)
            qs = stack_heads(q)
            us = stack_heads(u)
            total = qs.shape[0]
            p_low, ds_low, dq_t = [], [], []
            dq_rest = None
            for start in range(0, total, 2 * MAIN):
                stop = min(start + 2 * MAIN, total)
                s = dot_nt(k, qs[start:stop])
                dp = dot_nt(v, us[start:stop])
                e = jnp.exp2(s * (scaling * LOG2E) + bias_t[window, :, start:stop])
                p = e * (1.0 / jnp.sum(e, axis=0, keepdims=True))
                ds = p * (dp - jnp.sum(p * dp, axis=0, keepdims=True))
                if c == 0:
                    bias_acc[:, start:stop] = ds
                else:
                    bias_acc[:, start:stop] += ds
                p_low.append(p.astype(BF16))
                low = ds.astype(BF16)
                ds_low.append(low)
                if stop - start == 2 * MAIN:
                    head = start // MAIN
                    both = dot(k_t[head * head_dim : (head + 2) * head_dim], low)
                    dq_t += [both[:head_dim, :MAIN], both[head_dim:, MAIN:]]
                else:
                    flat = dot(jnp.transpose(ds).astype(BF16), k)
                    dq_rest = flat[:REM]
                    for head in range(1, heads):
                        dq_rest = jnp.where(
                            lane_head == head, flat[head * REM : (head + 1) * REM], dq_rest
                        )
            dq = jnp.concatenate([jnp.transpose(jnp.concatenate(dq_t, axis=0)), dq_rest], axis=0)
            dq = (dq * scaling).astype(BF16)
            dk = (dot(jnp.concatenate(ds_low, axis=1), qs) * scaling).astype(BF16)
            dv = dot(jnp.concatenate(p_low, axis=1), us).astype(BF16)
            scaled = (dot_nt(dq, wq) + dot_nt(dk, wk) + dot_nt(dv, wv)) * gain
            grads.append(
                inverse_rms
                * (
                    scaled
                    - jnp.mean(scaled, axis=-1, keepdims=True)
                    - standard * jnp.mean(scaled * standard, axis=-1, keepdims=True)
                )
            )
        for li, level in enumerate(at):
            rows = slice(li * LEVEL, (li + 1) * LEVEL)
            joined = jnp.concatenate([grad[rows] for grad in grads], axis=0).astype(BF16)
            spread = dot(perm_t[...], joined)
            base = 0
            for out, width in ((g_inner, cols), (g_below, cols), (g_right, SIDE), (g_corner, SIDE)):
                for row in range(HALF_ROWS):
                    out[level, row] = spread[base : base + width].astype(BF16)
                    base += width
        left = bias_acc[:, heads * MAIN :].astype(BF16)
        for head in range(heads):
            mine = bias_acc[:, head * MAIN : (head + 1) * MAIN].astype(BF16)
            turned = dot_nt(picks[:, :MAIN], mine) + dot_nt(picks[:, MAIN:] * rest_masks[head], left)
            for d in range(parts):
                chunks[d][window * heads + head] = turned[d * wide : d * wide + chunk].astype(BF16)
        return 0

    lax.fori_loop(0, level_windows, level_window, 0)


def join_kernel(g_inner, below, right, corner, *rest):
    chunks, (grad_input, bias_grad) = rest[:-2], rest[-2:]
    levels, _, cols, _ = g_inner.shape
    for level in range(levels):
        for row in range(HALF_ROWS):
            for base, wide, side in ((0, below, corner), (HALF_ROWS, g_inner, right)):
                whole = wide[level, row].astype(F32)
                first = whole[:SIDE] + side[level, row].astype(F32)
                joined = jnp.concatenate([first, whole[SIDE:]], axis=0)
                grad_input[level, base + row] = joined.astype(BF16)
    for i in range(bias_grad.shape[0]):
        total = chunks[0][i].astype(F32)
        for other in chunks[1:]:
            total += other[i].astype(F32)
        bias_grad[i] = total


def vmem(count):
    return [pl.BlockSpec(memory_space=pltpu.VMEM)] * count


def call(kernel, outs, args, flops=0, scratch=()):
    moved = sum(x.size * x.dtype.itemsize for x in list(args) + list(outs))
    return pl.pallas_call(
        kernel,
        out_shape=outs,
        in_specs=vmem(len(args)),
        out_specs=vmem(len(outs)),
        scratch_shapes=list(scratch),
        compiler_params=pltpu.CompilerParams(vmem_limit_bytes=40 * 2**20),
        cost_estimate=pl.CostEstimate(flops=flops, bytes_accessed=moved, transcendentals=0),
    )(*args)


def shift(value, rows, cols):
    lat_count, lon_count = lax.axis_size("lat"), lax.axis_size("lon")
    pairs = []
    for i in range(lat_count):
        for j in range(lon_count):
            to = (i + rows) % lat_count * lon_count + (j + cols) % lon_count
            pairs.append((i * lon_count + j, to))
    return lax.ppermute(value, ("lat", "lon"), pairs)


def local(tokens, cotangent, norm_gain, inproj_weight, outproj_weight, bias):
    levels, rows, cols, channels = tokens.shape
    level_windows, _, heads = bias.shape[:3]
    lat_count, lon_count = lax.axis_size("lat"), lax.axis_size("lon")
    chunk = WT // lon_count
    struct = jax.ShapeDtypeStruct

    wide = (HALF_ROWS, cols, channels)
    side = (HALF_ROWS, SIDE, channels)
    below, right, corner = call(
        send_kernel,
        [struct((2 * levels,) + shape, BF16) for shape in (wide, side, side)],
        (tokens, cotangent),
    )
    below = shift(below, -1, 0)
    right = shift(right, 0, -1)
    corner = shift(corner, -1, -1)
    bias_t, weights = call(
        functools.partial(prep_kernel, heads, lat_count),
        [
            struct((level_windows, WT, heads * WT), F32),
            struct((3, channels, channels), BF16),
        ],
        (bias.reshape(level_windows, heads, WT, WT), inproj_weight),
        flops=10**8,
    )
    order = window_order(cols)
    results = call(
        functools.partial(layer_kernel, heads, lon_count),
        [struct((levels,) + shape, BF16) for shape in (wide, wide, side, side)]
        + [struct((level_windows * heads, chunk, WT), BF16)] * lon_count,
        (
            tokens, cotangent, below, right, corner, norm_gain.reshape(1, channels),
            weights, outproj_weight, bias_t,
            jnp.asarray(order, BF16), jnp.asarray(order.T, BF16),
            jnp.asarray(query_choice(lon_count, heads), BF16),
        ),
        flops=10**9,
        scratch=[pltpu.VMEM((WT, heads * WT), F32)],
    )
    g_inner, g_below, g_right, g_corner = results[:4]
    chunks = results[4:]
    below = shift(g_below, 1, 0)
    right = shift(g_right, 0, 1)
    corner = shift(g_corner, 1, 1)
    arrived = [chunks[0]] + [shift(chunks[d], 0, d) for d in range(1, lon_count)]
    grad_input, bias_grad = call(
        join_kernel,
        [
            struct((levels, rows, cols, channels), BF16),
            struct((level_windows * heads, chunk, WT), F32),
        ],
        [g_inner, below, right, corner] + arrived,
    )
    return grad_input, bias_grad.reshape(level_windows, 1, heads, chunk, WT)


def solution(mesh):
    placed = (
        P(None, "lat", "lon", None),
        P(None, "lat", "lon", None),
        P(),
        P(),
        P(),
        P(None, "lat", None, None, None),
    )
    return jax.shard_map(
        local,
        mesh=mesh,
        in_specs=placed,
        out_specs=(P(None, "lat", "lon", None), P(None, "lat", None, "lon", None)),
        check_vma=False,
    )
```

time: 95 us -> 46.7 us (0.49)
  matrix products: 19.9 us -> 0 us
  between operations: 14.7 us -> 0.74 us
  local copies, waits for them, and re-layouts: 17.3 us -> 5.58 us
  Pallas kernels: 0 us -> 9.83 us
  other arithmetic: 8.53 us -> 0 us
  waiting for transfers between devices: 21.4 us -> 18 us
    reduce_scatter x1 -> x0, waiting for transfers between devices: 15.8 us -> none  [local(): lax.psum_scatter(bias_local.astype(jnp.bfloat16), 'lon', scatter_dimensio...]
    dot_general x14 -> x0, matrix products: 12.5 us -> none  [the longest x2 4.65 us: band_backward(): jnp.einsum('nhij,nihd->njhd', probs_low, upstream, preferred_element_type...]
    ppermute x8 -> x9, waiting for transfers between devices: 5.57 us -> 18 us  [shift(): return lax.ppermute(value, ('lat', 'lon'), pairs)]
    pallas_call x0 -> x4, Pallas kernels: none -> 9.83 us  [call(): pl.pallas_call(kernel, out_shape=outs, in_specs=vmem(len(args)), out_spec...]
    div x2 -> x0, matrix products: 7.31 us -> none  [band_backward(): probabilities = weights / jnp.sum(weights, axis=-1, keepdims=True)]
    slice x10 -> x0, local copies, waits for them, and re-layouts: 3.92 us -> none  [the longest x2 2.47 us: band_backward(): value_rows = projected[:, :, 2]]
    add x3 -> x0, local copies, waits for them, and re-layouts: 2.83 us -> none  [band_backward(): jnp.einsum('nihd,njhd->nhij', query_rows, key_rows, preferred_element_typ...]
    another operation x5 -> x0, other arithmetic: 2.82 us -> none  [the longest x2 2.36 us: local(): stacked = jnp.stack([tokens, cotangent])]
  transfers between devices with their start and end apart: 9 -> 9, of which waited for: 4 -> 3; matrix products, arithmetic and copies ran while one was open for 9% -> 0% of each run, Pallas kernels for 0% -> 1%
where the time goes in v1:
time: 46.7 us; the launch traced here: 46.4 us
  waiting for transfers between devices  18 us (39%)
  starting transfers between devices  12.3 us (26%)
  Pallas kernels  9.83 us (21%)
  local copies, waits for them, and re-layouts  5.58 us (12%)
  between operations  0.74 us (2%)
    ppermute x9, waiting for transfers between devices, shift(): return lax.ppermute(value, ('lat', 'lon'), pairs)  18 us
    ppermute x9, starting transfers between devices, shift(): return lax.ppermute(value, ('lat', 'lon'), pairs)  12.3 us
    pallas_call x4, Pallas kernels, call(): pl.pallas_call(kernel, out_shape=outs, in_specs=vmem(len(args)), out_spec...  9.83 us
    unnamed x23, local copies, waits for them, and re-layouts  5.58 us
  transfers between devices with their start and end apart: 9, of which 3 were waited for; matrix products, arithmetic and copies ran while one was open for 0% of the time, Pallas kernels for 1%

profile of v1, /device:TPU:0, one launch (start us, length us, event | category | flops | bytes accessed | tf_op | source)
XLA Modules:
  0.0 46.4 jit_solution(16448400004787827711)
XLA Ops:
  0.6 0.0 copy-start.1
  0.6 1.0 %copy-done.1 = bf16[4,6,24,192]{3,2,1,0:T(8,128)(2,1)S(1)} copy-done((bf16[4,6,24,192]{3,2,1,0:T(8,128)(2,1)S(1)}, bf16[4,6,24,192]{3,2,1,0:T(8,128)(2,1)}, u32[]{:S(2)}) %copy-start.1) | copy-done | bytes 221208
  1.6 0.0 copy-start.3
  1.6 1.0 %copy-done.3 = bf16[4,6,24,192]{3,2,1,0:T(8,128)(2,1)S(1)} copy-done((bf16[4,6,24,192]{3,2,1,0:T(8,128)(2,1)S(1)}, bf16[4,6,24,192]{3,2,1,0:T(8,128)(2,1)}, u32[]{:S(2)}) %copy-start.3) | copy-done | bytes 221208
  2.6 0.0 copy-start.2
  2.6 0.0 copy-start.4
  2.6 0.0 copy-start.7
  2.6 4.5 %collective-permute-start = (bf16[8,3,24,192]{3,2,1,0:T(8,128)(2,1)S(1)}, bf16[8,3,24,192]{3,2,1,0:T(8,128)(2,1)S(1)}, u32[]{:S(2)}, u32[]{:S(2)}) collective-permute-start(bf16[8,3,24,192]{3,2,1,0:T(8,128)(2,1)S(1)} %get-tuple-element.17), channel_id=1, source_target_pairs={{0,28},{1,29},{2,30},{3,31},{4,0},{5,1},{6,2},{7,3},{8,4},{9,5},{1... | collective-permute-start | bytes 663560 | tf_op jit(solution)/shard_map/ppermute | solution.py:268
  7.1 2.4 %collective-permute-start.1 = (bf16[8,3,8,192]{3,2,1,0:T(8,128)(2,1)S(1)}, bf16[8,3,8,192]{3,2,1,0:T(8,128)(2,1)S(1)}, u32[]{:S(2)}, u32[]{:S(2)}) collective-permute-start(bf16[8,3,8,192]{3,2,1,0:T(8,128)(2,1)S(1)} %get-tuple-element.18), channel_id=1, source_target_pairs={{0,3},{1,0},{2,1},{3,2},{4,7},{5,4},{6,5},{7,6},{8,11},{9,8},{10,9... | collective-permute-start | bytes 221192 | tf_op jit(solution)/shard_map/ppermute | solution.py:268
  9.6 0.4 collective-permute-start.2
  10.0 0.0 copy-start
  10.0 1.5 %copy-done = f32[2,1,6,144,144]{4,3,2,1,0:T(8,128)S(1)} copy-done((f32[2,1,6,144,144]{4,3,2,1,0:T(8,128)S(1)}, f32[2,1,6,144,144]{4,3,2,1,0:T(8,128)}, u32[]{:S(2)}) %copy-start) | copy-done | bytes 995352
  11.4 0.0 copy-start.5
  11.4 0.9 %copy-done.5 = bf16[192,576]{1,0:T(8,128)(2,1)S(1)} copy-done((bf16[192,576]{1,0:T(8,128)(2,1)S(1)}, bf16[192,576]{1,0:T(8,128)(2,1)}, u32[]{:S(2)}) %copy-start.5) | copy-done | bytes 221208
  12.4 0.0 copy-start.6
  12.4 0.0 copy-start.8
  12.4 0.0 copy-start.9
  12.4 0.0 copy-start.10
  12.4 0.6 %shard_map.105 = (f32[2,144,864]{2,1,0:T(8,128)S(1)}, bf16[3,192,192]{2,1,0:T(8,128)(2,1)S(1)}) custom-call(f32[2,6,144,144]{3,2,1,0:T(8,128)S(1)} %bitcast.3, bf16[192,576]{1,0:T(8,128)(2,1)S(1)} %copy-done.5), custom_call_target="tpu_custom_call" | custom-call | flops 100000000 | bytes 2433024 | tf_op jit(solution)/shard_map/pallas_call | solution.py:250
  13.0 0.0 collective-permute-done.1.right
  13.0 0.9 %collective-permute-done.2.corner = bf16[8,3,8,192]{3,2,1,0:T(8,128)(2,1)S(1)} collective-permute-done((bf16[8,3,8,192]{3,2,1,0:T(8,128)(2,1)S(1)}, bf16[8,3,8,192]{3,2,1,0:T(8,128)(2,1)S(1)}, u32[]{:S(2)}, u32[]{:S(2)}) %collective-permute-start.2) | collective-permute-done | bytes 73760 | tf_op jit(solution)/shard_map/ppermute | solution.py:268
  13.9 0.0 collective-permute-done.below
  13.9 0.0 copy-done.2
  13.9 0.0 copy-done.4
  13.9 0.0 copy-done.7
  13.9 0.0 copy-done.6
  13.9 0.0 copy-done.8
  13.9 0.0 copy-done.9
  13.9 0.0 copy-done.10
  13.9 8.4 %shard_map.106 = (bf16[4,3,24,192]{3,2,1,0:T(8,128)(2,1)S(1)}, bf16[4,3,24,192]{3,2,1,0:T(8,128)(2,1)S(1)}, bf16[4,3,8,192]{3,2,1,0:T(8,128)(2,1)S(1)}, bf16[4,3...) custom-call(bf16[4,6,24,192]{3,2,1,0:T(8,128)(2,1)S(1)} %copy-done.2, ...), custom_call_target="tpu_custom_call" | custom-call | flops 1000000000 | bytes 3091200 | tf_op jit(solution)/shard_map/pallas_call | solution.py:250
  22.4 2.2 %collective-permute-start.6 = (bf16[12,36,144]{2,1,0:T(8,128)(2,1)S(1)}, bf16[12,36,144]{2,1,0:T(8,128)(2,1)S(1)}, u32[]{:S(2)}, u32[]{:S(2)}) collective-permute-start(bf16[12,36,144]{2,1,0:T(8,128)(2,1)S(1)} %get-tuple-element.27), channel_id=1, source_target_pairs={{0,1},{1,2},{2,3},{3,0},{4,5},{5,6},{6,7},{7,4},{8,9},{9,10},{10,1... | collective-permute-start | bytes 373256 | tf_op jit(solution)/shard_map/ppermute | solution.py:268
  24.5 0.7 %collective-permute-start.7 = (bf16[12,36,144]{2,1,0:T(8,128)(2,1)S(1)}, bf16[12,36,144]{2,1,0:T(8,128)(2,1)S(1)}, u32[]{:S(2)}, u32[]{:S(2)}) collective-permute-start(bf16[12,36,144]{2,1,0:T(8,128)(2,1)S(1)} %get-tuple-element.28), channel_id=1, source_target_pairs={{0,2},{1,3},{2,0},{3,1},{4,6},{5,7},{6,4},{7,5},{8,10},{9,11},{10,... | collective-permute-start | bytes 373256 | tf_op jit(solution)/shard_map/ppermute | solution.py:268
  25.3 1.6 %collective-permute-start.8 = (bf16[12,36,144]{2,1,0:T(8,128)(2,1)S(1)}, bf16[12,36,144]{2,1,0:T(8,128)(2,1)S(1)}, u32[]{:S(2)}, u32[]{:S(2)}) collective-permute-start(bf16[12,36,144]{2,1,0:T(8,128)(2,1)S(1)} %get-tuple-element.29), channel_id=1, source_target_pairs={{0,3},{1,0},{2,1},{3,2},{4,7},{5,4},{6,5},{7,6},{8,11},{9,8},{10,9... | collective-permute-start | bytes 373256 | tf_op jit(solution)/shard_map/ppermute | solution.py:268
  26.9 0.0 collective-permute-start.3
  26.9 0.4 collective-permute-start.4
  27.3 10.0 %collective-permute-done.4.right = bf16[4,3,8,192]{3,2,1,0:T(8,128)(2,1)S(1)} collective-permute-done((bf16[4,3,8,192]{3,2,1,0:T(8,128)(2,1)S(1)}, bf16[4,3,8,192]{3,2,1,0:T(8,128)(2,1)S(1)}, u32[]{:S(2)}, u32[]{:S(2)}) %collective-permute-start.4) | collective-permute-done | bytes 36896 | tf_op jit(solution)/shard_map/ppermute | solution.py:268
  37.3 0.0 collective-permute-start.5
  37.3 7.1 %collective-permute-done.5.corner = bf16[4,3,8,192]{3,2,1,0:T(8,128)(2,1)S(1)} collective-permute-done((bf16[4,3,8,192]{3,2,1,0:T(8,128)(2,1)S(1)}, bf16[4,3,8,192]{3,2,1,0:T(8,128)(2,1)S(1)}, u32[]{:S(2)}, u32[]{:S(2)}) %collective-permute-start.5) | collective-permute-done | bytes 36896 | tf_op jit(solution)/shard_map/ppermute | solution.py:268
  44.4 0.0 collective-permute-done.3.below
  44.4 0.0 collective-permute-done.6.rest_1_
  44.4 0.0 collective-permute-done.7.rest_2_
  44.4 0.0 collective-permute-done.8.rest_3_
  44.4 0.8 %shard_map.107 = (bf16[4,6,24,192]{3,2,1,0:T(8,128)(2,1)}, f32[12,36,144]{2,1,0:T(8,128)S(1)}) custom-call(bf16[4,3,24,192]{3,2,1,0:T(8,128)(2,1)S(1)} %get-tuple-element.22.g_inner, bf16[4,3,24,192]{3,2,1,0:T(8,128)(2,1)S(1)} %collective-permute-done.3.below, bf16[4,3,8,192]{3,2,1,0:T(8,128)(2,1)S(1)} %collective-permute-done.4.right, ...), custom_call_target="tpu_custom_call" | custom-call | bytes 1262592 | tf_op jit(solution)/shard_map/pallas_call | solution.py:250
  45.2 1.2 %copy.11 = f32[2,1,6,36,144]{4,1,3,2,0:T(1,128)} copy(f32[2,1,6,36,144]{4,3,2,0,1:T(8,128)S(1)} %bitcast.4) | data formatting | bytes 497664
  (1 shorter events, 0.0 us)
Async XLA Ops:
  0.6 1.0 %copy-start.1 = (bf16[4,6,24,192]{3,2,1,0:T(8,128)(2,1)S(1)}, bf16[4,6,24,192]{3,2,1,0:T(8,128)(2,1)}, u32[]{:S(2)}) copy-start(bf16[4,6,24,192]{3,2,1,0:T(8,128)(2,1)} %tok.3) | copy-start | bytes 663556
  1.6 1.0 %copy-start.3 = (bf16[4,6,24,192]{3,2,1,0:T(8,128)(2,1)S(1)}, bf16[4,6,24,192]{3,2,1,0:T(8,128)(2,1)}, u32[]{:S(2)}) copy-start(bf16[4,6,24,192]{3,2,1,0:T(8,128)(2,1)} %cot.3) | copy-start | bytes 663556
  2.6 11.3 %copy-start.2 = (bf16[4,6,24,192]{3,2,1,0:T(8,128)(2,1)S(1)}, bf16[4,6,24,192]{3,2,1,0:T(8,128)(2,1)}, u32[]{:S(2)}) copy-start(bf16[4,6,24,192]{3,2,1,0:T(8,128)(2,1)} %tok.3) | copy-start | bytes 663556
  2.6 11.3 %copy-start.4 = (bf16[4,6,24,192]{3,2,1,0:T(8,128)(2,1)S(1)}, bf16[4,6,24,192]{3,2,1,0:T(8,128)(2,1)}, u32[]{:S(2)}) copy-start(bf16[4,6,24,192]{3,2,1,0:T(8,128)(2,1)} %cot.3) | copy-start | bytes 663556
  2.6 11.3 %copy-start.7 = (f32[192]{0:T(256)S(1)}, f32[192]{0:T(256)}, u32[]{:S(2)}) copy-start(f32[192]{0:T(256)} %param.11) | copy-start | bytes 2308
  2.6 11.3 %collective-permute-start = (bf16[8,3,24,192]{3,2,1,0:T(8,128)(2,1)S(1)}, bf16[8,3,24,192]{3,2,1,0:T(8,128)(2,1)S(1)}, u32[]{:S(2)}, u32[]{:S(2)}) collective-permute-start(bf16[8,3,24,192]{3,2,1,0:T(8,128)(2,1)S(1)} %get-tuple-element.17), channel_id=1, source_target_pairs={{0,28},{1,29},{2,30},{3,31},{4,0},{5,1},{6,2},{7,3},{8,4},{9,5},{1... | collective-permute-start | bytes 663560 | tf_op jit(solution)/shard_map/ppermute | solution.py:268
  7.1 5.8 %collective-permute-start.1 = (bf16[8,3,8,192]{3,2,1,0:T(8,128)(2,1)S(1)}, bf16[8,3,8,192]{3,2,1,0:T(8,128)(2,1)S(1)}, u32[]{:S(2)}, u32[]{:S(2)}) collective-permute-start(bf16[8,3,8,192]{3,2,1,0:T(8,128)(2,1)S(1)} %get-tuple-element.18), channel_id=1, source_target_pairs={{0,3},{1,0},{2,1},{3,2},{4,7},{5,4},{6,5},{7,6},{8,11},{9,8},{10,9... | collective-permute-start | bytes 221192 | tf_op jit(solution)/shard_map/ppermute | solution.py:268
  9.6 4.3 %collective-permute-start.2 = (bf16[8,3,8,192]{3,2,1,0:T(8,128)(2,1)S(1)}, bf16[8,3,8,192]{3,2,1,0:T(8,128)(2,1)S(1)}, u32[]{:S(2)}, u32[]{:S(2)}) collective-permute-start(bf16[8,3,8,192]{3,2,1,0:T(8,128)(2,1)S(1)} %get-tuple-element.19), channel_id=1, source_target_pairs={{0,31},{1,28},{2,29},{3,30},{4,3},{5,0},{6,1},{7,2},{8,7},{9,4},{1... | collective-permute-start | bytes 221192 | tf_op jit(solution)/shard_map/ppermute | solution.py:268
  10.0 1.5 %copy-start = (f32[2,1,6,144,144]{4,3,2,1,0:T(8,128)S(1)}, f32[2,1,6,144,144]{4,3,2,1,0:T(8,128)}, u32[]{:S(2)}) copy-start(f32[2,1,6,144,144]{4,3,2,1,0:T(8,128)} %param.14) | copy-start | bytes 2985988
  11.4 0.9 %copy-start.5 = (bf16[192,576]{1,0:T(8,128)(2,1)S(1)}, bf16[192,576]{1,0:T(8,128)(2,1)}, u32[]{:S(2)}) copy-start(bf16[192,576]{1,0:T(8,128)(2,1)} %inproj.1) | copy-start | bytes 663556
  12.4 1.5 %copy-start.6 = (bf16[192,192]{1,0:T(8,128)(2,1)S(1)}, bf16[192,192]{1,0:T(8,128)(2,1)}, u32[]{:S(2)}) copy-start(bf16[192,192]{1,0:T(8,128)(2,1)} %outproj.1) | copy-start | bytes 221188
  12.4 1.5 %copy-start.8 = (bf16[4,48,224]{2,1,0:T(8,128)(2,1)S(1)}, bf16[4,48,224]{2,1,0:T(8,128)(2,1)}, u32[]{:S(2)}) copy-start(bf16[4,48,224]{2,1,0:T(8,128)(2,1)} %constant.8.clone.choice) | copy-start | bytes 258052
  12.4 1.5 %copy-start.9 = (bf16[192,144]{1,0:T(8,128)(2,1)S(1)}, bf16[192,144]{1,0:T(8,128)(2,1)}, u32[]{:S(2)}) copy-start(bf16[192,144]{1,0:T(8,128)(2,1)} %constant.7.clone.perm_t) | copy-start | bytes 165892
  12.4 1.5 %copy-start.10 = (bf16[144,192]{1,0:T(8,128)(2,1)S(1)}, bf16[144,192]{1,0:T(8,128)(2,1)}, u32[]{:S(2)}) copy-start(bf16[144,192]{1,0:T(8,128)(2,1)} %constant.6.clone.perm) | copy-start | bytes 165892
  22.4 22.1 %collective-permute-start.6 = (bf16[12,36,144]{2,1,0:T(8,128)(2,1)S(1)}, bf16[12,36,144]{2,1,0:T(8,128)(2,1)S(1)}, u32[]{:S(2)}, u32[]{:S(2)}) collective-permute-start(bf16[12,36,144]{2,1,0:T(8,128)(2,1)S(1)} %get-tuple-element.27), channel_id=1, source_target_pairs={{0,1},{1,2},{2,3},{3,0},{4,5},{5,6},{6,7},{7,4},{8,9},{9,10},{10,1... | collective-permute-start | bytes 373256 | tf_op jit(solution)/shard_map/ppermute | solution.py:268
  24.5 19.9 %collective-permute-start.7 = (bf16[12,36,144]{2,1,0:T(8,128)(2,1)S(1)}, bf16[12,36,144]{2,1,0:T(8,128)(2,1)S(1)}, u32[]{:S(2)}, u32[]{:S(2)}) collective-permute-start(bf16[12,36,144]{2,1,0:T(8,128)(2,1)S(1)} %get-tuple-element.28), channel_id=1, source_target_pairs={{0,2},{1,3},{2,0},{3,1},{4,6},{5,7},{6,4},{7,5},{8,10},{9,11},{10,... | collective-permute-start | bytes 373256 | tf_op jit(solution)/shard_map/ppermute | solution.py:268
  25.3 19.2 %collective-permute-start.8 = (bf16[12,36,144]{2,1,0:T(8,128)(2,1)S(1)}, bf16[12,36,144]{2,1,0:T(8,128)(2,1)S(1)}, u32[]{:S(2)}, u32[]{:S(2)}) collective-permute-start(bf16[12,36,144]{2,1,0:T(8,128)(2,1)S(1)} %get-tuple-element.29), channel_id=1, source_target_pairs={{0,3},{1,0},{2,1},{3,2},{4,7},{5,4},{6,5},{7,6},{8,11},{9,8},{10,9... | collective-permute-start | bytes 373256 | tf_op jit(solution)/shard_map/ppermute | solution.py:268
  26.9 17.6 %collective-permute-start.3 = (bf16[4,3,24,192]{3,2,1,0:T(8,128)(2,1)S(1)}, bf16[4,3,24,192]{3,2,1,0:T(8,128)(2,1)S(1)}, u32[]{:S(2)}, u32[]{:S(2)}) collective-permute-start(bf16[4,3,24,192]{3,2,1,0:T(8,128)(2,1)S(1)} %get-tuple-element.23), channel_id=1, source_target_pairs={{0,4},{1,5},{2,6},{3,7},{4,8},{5,9},{6,10},{7,11},{8,12},{9,13},{1... | collective-permute-start | bytes 331784 | tf_op jit(solution)/shard_map/ppermute | solution.py:268
  26.9 10.4 %collective-permute-start.4 = (bf16[4,3,8,192]{3,2,1,0:T(8,128)(2,1)S(1)}, bf16[4,3,8,192]{3,2,1,0:T(8,128)(2,1)S(1)}, u32[]{:S(2)}, u32[]{:S(2)}) collective-permute-start(bf16[4,3,8,192]{3,2,1,0:T(8,128)(2,1)S(1)} %get-tuple-element.24), channel_id=1, source_target_pairs={{0,1},{1,2},{2,3},{3,0},{4,5},{5,6},{6,7},{7,4},{8,9},{9,10},{10,1... | collective-permute-start | bytes 110600 | tf_op jit(solution)/shard_map/ppermute | solution.py:268
  37.3 7.1 %collective-permute-start.5 = (bf16[4,3,8,192]{3,2,1,0:T(8,128)(2,1)S(1)}, bf16[4,3,8,192]{3,2,1,0:T(8,128)(2,1)S(1)}, u32[]{:S(2)}, u32[]{:S(2)}) collective-permute-start(bf16[4,3,8,192]{3,2,1,0:T(8,128)(2,1)S(1)} %get-tuple-element.25), channel_id=1, source_target_pairs={{0,5},{1,6},{2,7},{3,4},{4,9},{5,10},{6,11},{7,8},{8,13},{9,14},{1... | collective-permute-start | bytes 110600 | tf_op jit(solution)/shard_map/ppermute | solution.py:268
